TPU v7x, 32 devices: a whole 2x2x4 slice. The times are simulated.
32 devices in a mesh: ctx: 16 (over z, y, core), head: 2 (over x).
Axes of the slice: x: 2, y: 2, z: 4, core: 2. Of those that a mesh axis runs over, the one named last changes fastest.
Arguments:
- queries: bfloat16 [8192, 4096], P('ctx', 'head'), may hold values from -48 to 48
- keys: bfloat16 [8192, 1024], P('ctx', 'head'), may hold values from -4 to 4
- values: bfloat16 [8192, 1024], P('ctx', 'head'), may hold values from -6 to 6
- doc_start: int32 [8192], P('ctx'), may hold values from 0 to 8191, as said below
- out_weight: bfloat16 [4096, 4096], P('head'), may hold values from -0.09375 to 0.09375
Outputs:
- mixed: bfloat16 [8192, 4096], P(('ctx', 'head'))
Inputs may be any that keep to these rules, and one draw needn't show every extreme that they name: doc_start is non-decreasing, doc_start[i] <= i, and all tokens of a document share its first position; every document has at most 4096 tokens and one document has exactly 4096; the 4096-token document starts at a multiple of 1024, and all other documents lie inside aligned cells of 1024 tokens.
All inputs are finite; a program needn't handle non-finite values.
Results may differ from a plain program's by a relative error of at most 0.015.
Values may be sent and summed in bfloat16 or wider, within the bound.
A program may use at most 448 MiB of HBM per device.

v0:
```python
import jax
import jax.numpy as jnp
from jax import lax
from jax.sharding import PartitionSpec as P

HD = 128
GROUP = 4


NEG_FILL = -1e30


def attend_block(state, queries, keys, values, key_start, doc_rows, query_pos):
    count = keys.shape[0]
    kv_heads = queries.shape[1]
    key_pos = jnp.arange(count, dtype=jnp.int32)
    needed = (key_start + count - 1 >= doc_rows[0]) & (key_start <= query_pos[-1])

    def compute(carry):
        running, total, accum = carry
        key_tile = keys.reshape(count, kv_heads, HD)
        value_tile = values.reshape(count, kv_heads, HD)
        scores = jnp.einsum(
            "tkgd,skd->kgts", queries, key_tile, preferred_element_type=jnp.float32
        ) * HD ** (-0.5)
        allowed = (key_pos[None, :] >= doc_rows[:, None]) & (key_pos[None, :] <= query_pos[:, None])
        scores = jnp.where(allowed, scores, NEG_FILL)
        newmax = jnp.maximum(running, jnp.max(scores, axis=-1))
        weights = jnp.where(allowed, jnp.exp(scores - newmax[..., None]), 0.0)
        total = jnp.sum(weights, axis=-1)
        low_weight = weights.astype(jnp.bfloat16)
        accum = jnp.einsum(
            "kgts,skd->kgtd", low_weight, value_tile, preferred_element_type=jnp.float32
        )
        return (newmax, total, accum)

    return lax.cond(needed, compute, lambda carry: carry, state)


def on_device(queries, keys, values, doc_start, out_weight):
    tok_rows = queries.shape[0]
    kv_heads = keys.shape[1] // HD
    my_index = lax.axis_index("ctx")
    query_pos = my_index * tok_rows + jnp.arange(tok_rows, dtype=jnp.int32)
    grouped = queries.reshape(tok_rows, kv_heads, GROUP, HD)
    initial = (
        jnp.full((kv_heads, GROUP, tok_rows), NEG_FILL, jnp.float32),
        jnp.zeros((kv_heads, GROUP, tok_rows), jnp.float32),
        jnp.zeros((kv_heads, GROUP, tok_rows, HD), jnp.float32),
    )
    stacked = jnp.stack([keys, values])
    tile = lax.all_gather(stacked, "ctx", axis=1, tiled=True)
    state = attend_block(initial, grouped, tile[0], tile[1], jnp.int32(0), doc_start, query_pos)
    running, total, accum = state
    attended = (
        (accum / total[..., None])
        .transpose(2, 0, 1, 3)
        .reshape(tok_rows, kv_heads * GROUP * HD)
        .astype(jnp.bfloat16)
    )
    return lax.psum_scatter(
        jnp.dot(attended, out_weight, preferred_element_type=jnp.float32).astype(jnp.bfloat16),
        "head",
        scatter_dimension=0,
        tiled=True,
    )


def solution(mesh):
    return jax.shard_map(
        on_device,
        mesh=mesh,
        in_specs=(P("ctx", "head"), P("ctx", "head"), P("ctx", "head"), P("ctx"), P("head", None)),
        out_specs=P(("ctx", "head"), None),
        check_vma=False,
    )
```

profile of v0, /device:TPU:17, one launch (start us, length us, event | category | flops | bytes accessed | tf_op | source)
XLA Modules:
  0.0 510.8 jit_solution(12836356377978278664)
XLA Ops:
  6.5 0.0 all-gather.2.cloned.1.call-start
  6.5 1.3 copy.13
  7.8 1.3 copy.14
  9.1 1.1 pad_maximum_fusion
  10.1 0.0 all-gather.2.cloned.1.call-update
  10.1 0.0 reduce-scatter.2.cloned.1.call-start
  10.2 1.2 slice.14
  11.4 0.6 slice.15
  13.3 127.9 %all-gather.2.cloned.1.call-done = bf16[2,8192,512]{1,2,0:T(8,128)(2,1)} async-done(((bf16[2,512,512]{1,2,0:T(8,128)(2,1)}), bf16[2,8192,512]{1,2,0:T(8,128)(2,1)}) %all-gather.2.cloned.1.call-update) | async-done | bytes 16777232 | tf_op jit(solution)/shard_map/all_gather | solution.py:52
  141.2 292.9 %conditional.1 = (f32[4,4,512]{2,1,0:T(4,128)}, f32[4,4,512,128]{2,3,1,0:T(8,128)}) conditional(s32[]{:T(128)} %bitcast.5, () %tuple.13, (s32[8192]{0:T(1024)S(1)}, s32[8192]{0:T(1024)S(1)}, s32[512]{0:T(512)}, s32[512]{0:T(512)S(1)}, bf16[2,8192,512]{1,2,0:T(8,128)(2,1)}, /*index=5*/bf16[512,2048]{1,0:T(8,128)(2,1)}) %tuple.14), branch_computations={%region_0.0_spmd, %region_1.4_spmd} | conditional | flops 35244728320 | bytes 883167232 | solution.py:37
  141.2 3.2 reshape.19
  144.5 7.8 %compare_and_fusion = pred[512,8192]{0,1:T(8,128)(4,1)} fusion(s32[512]{0:T(512)S(1)} %get-tuple-element.23, s32[512]{0:T(512)} %get-tuple-element.21, s32[8192]{0:T(1024)S(1)} %get-tuple-element.22, s32[8192]{0:T(1024)S(1)} %get-tuple-element.22), kind=kLoop, calls=%fused_computation.7 | loop fusion | flops 12582912 | bytes 4263936 | tf_op jit(solution)/shard_map/cond/branch_1_fun/and | solution.py:26
  152.3 11.6 %fusion.11 = (bf16[1,8192,512]{1,2,0:T(8,128)(2,1)}, bf16[1,8192,512]{1,2,0:T(8,128)(2,1)}) fusion(bf16[2,8192,512]{1,2,0:T(8,128)(2,1)} %get-tuple-element.24), kind=kLoop, calls=%fused_computation.18 | loop fusion | bytes 33554432 | tf_op jit(solution)/shard_map/slice | solution.py:53
  163.8 91.5 %fusion = (f32[4,4,512]{2,1,0:T(4,128)S(1)}, f32[4,8192,512,4]{2,1,3,0:T(8,128)}) fusion(pred[512,8192]{0,1:T(8,128)(4,1)} %compare_and_fusion, bf16[8192,4,128,1]{0,2,3,1:T(8,128)(2,1)} %bitcast.32, bf16[512,4,4,128]{3,2,1,0:T(4,128)(2,1)S(1)} %reshape.19), kind=kOutput, calls=%fused_computation.2 | convolution fusion | flops 17381187584 | bytes 283148288 | tf_op jit(solution)/shard_map/cond/branch_1_fun/tkgd,skd->kgts/dot_general | solution.py:23
  255.3 96.1 %fusion.3 = f32[4,4,512,128]{2,3,1,0:T(8,128)} fusion(bf16[8192,4,128,1]{0,2,3,1:T(8,128)(2,1)} %bitcast.31, f32[4,8192,512,4]{2,1,3,0:T(8,128)} %get-tuple-element.36, f32[4,4,512]{2,1,0:T(4,128)S(1)} %broadcast_maximum_fusion, pred[512,8192]{0,1:T(8,128)(4,1)} %compare_and_fusion), kind=kOutput, calls=%fused_computation.5 | convolution fusion | flops 17515413504 | bytes 285245440 | tf_op jit(solution)/shard_map/cond | solution.py:37
  351.5 82.6 %fusion.2 = f32[4,4,512]{2,1,0:T(4,128)} fusion(f32[4,8192,512,4]{2,1,3,0:T(8,128)} %get-tuple-element.36, f32[4,4,512]{2,1,0:T(4,128)S(1)} %broadcast_maximum_fusion, pred[512,8192]{0,1:T(8,128)(4,1)} %compare_and_fusion), kind=kLoop, calls=%fused_computation.4 | loop fusion | flops 335536128 | bytes 272695296 | tf_op jit(solution)/shard_map/cond/branch_1_fun/reduce_sum | solution.py:30
  434.1 2.8 divide_convert_fusion
  436.9 13.9 %convolution_convert_fusion = bf16[512,4096]{1,0:T(8,128)(2,1)} fusion(bf16[512,2048]{0,1:T(8,128)(2,1)S(1)} %bitcast.33, bf16[2048,4096]{1,0:T(8,128)(2,1)} %param.11), kind=kOutput, calls=%fused_computation.14 | convolution fusion | flops 8592031744 | bytes 23068672 | tf_op jit(solution)/shard_map/dot_general | solution.py:62
  450.8 0.0 reduce-scatter.2.cloned.1.call-update
  450.8 53.1 %reduce-scatter.2.cloned.1.call-done = bf16[256,4096]{1,0:T(8,128)(2,1)} async-done(((bf16[512,4096]{1,0:T(8,128)(2,1)}), bf16[256,4096]{1,0:T(8,128)(2,1)}) %reduce-scatter.2.cloned.1.call-update) | async-done | bytes 2097168 | tf_op jit(solution)/shard_map/reduce_scatter | solution.py:61
  (3 shorter events, 0.0 us)
Async XLA Ops:
  6.5 134.7 %all-gather.2.cloned.1.call-start = ((), (), s32[]{:S(2)}) async-start(), calls=%async_computation.1 | async-start | bytes 17825792 | tf_op jit(solution)/shard_map/all_gather | solution.py:52
  10.1 493.8 %reduce-scatter.2.cloned.1.call-start = ((), (), s32[]{:S(2)}) async-start(), calls=%async_computation.2 | async-start | bytes 6291456 | tf_op jit(solution)/shard_map/reduce_scatter | solution.py:61
Sparse Core Ops, SparseCore 0:
  10.3 130.9 all-gather.1
  451.0 52.9 reduce-scatter.1
where the time goes:
time: 513 us; the launch traced here: 511 us
  matrix products  202 us (39%)
  waiting for transfers between devices  181 us (35%)
  other arithmetic  94.3 us (18%)
  local copies, waits for them, and re-layouts  19.2 us (4%)
  between operations  14.7 us (3%)
    all_gather x1, waiting for transfers between devices, on_device(): tile = lax.all_gather(stacked, 'ctx', axis=1, tiled=True)  128 us
    cond x1, matrix products, attend_block(): return lax.cond(needed, compute, lambda carry: carry, state)  96.1 us
    dot_general x1, matrix products, compute(): jnp.einsum('tkgd,skd->kgts', queries, key_tile, preferred_element_type=jn...  91.5 us
    reduce_sum x1, other arithmetic, compute(): total = jnp.sum(weights, axis=-1)  82.6 us
    reduce_scatter x1, waiting for transfers between devices, on_device(): lax.psum_scatter(jnp.dot(attended, out_weight, preferred_element_type=jnp...  53.1 us
    dot_general x1, matrix products, on_device(): jnp.dot(attended, out_weight, preferred_element_type=jnp.float32)  13.9 us
    slice x1, local copies, waits for them, and re-layouts, on_device(): tile[1]  11.6 us
  transfers between devices with their start and end apart: 2, of which 2 were waited for; matrix products, arithmetic and copies ran while one was open for 0% of the time, Pallas kernels for 0%

commit v1 on v0

v1 whole, which is shorter than its diff:
```python
import functools

import jax
import jax.numpy as jnp
from jax import lax
from jax.experimental import pallas as pl
from jax.experimental.pallas import tpu as pltpu
from jax.sharding import PartitionSpec as P

HD = 128
GROUP = 4
LONGEST = 4096
SHORT = 1024
CORES = 2
NEG_FILL = -1e30
POS_FILL = 1e30
SCALE = HD ** -0.5 * 1.4426950408889634
MESH = pl.DeviceIdType.MESH
PIECES = 2


def wide(x, count):
    return jnp.concatenate([x] * count, axis=1)


def kernel(
    n_ctx, n_head, n_slots, chunk,
    q_hbm, k_hbm, v_hbm, doc_ref, w_hbm, out_ref,
    q_ref, own, sib, slots, w_ref, acc, top, att, outbox, inbox,
    load_sem, send_sem, recv_sem, psend_sem, precv_sem,
):
    me = lax.axis_index("ctx")
    head = lax.axis_index("head")
    chip, core = me // CORES, lax.rem(me, CORES)
    chips = n_ctx // CORES
    side = lax.rem(chip, 2)
    sibling = chip * CORES + (1 - core)
    beside = (chip + 1 - 2 * side) * CORES + core
    ahead = me + 2 * CORES
    behind = me - 2 * CORES
    rows = q_ref.shape[0]
    q_heads = q_ref.shape[1] // HD
    part = rows // n_head
    width = w_ref.shape[1]

    loads = [
        pltpu.make_async_copy(src, dst, load_sem.at[n])
        for n, (src, dst) in enumerate(
            [(q_hbm, q_ref), (k_hbm, own.at[0]), (v_hbm, own.at[1]), (w_hbm, w_ref)]
        )
    ]
    for load in loads:
        load.start()

    barrier = pltpu.get_barrier_semaphore()
    has_ahead = chip + 2 < chips
    has_behind = chip >= 2

    def greet(target):
        pl.semaphore_signal(barrier, inc=1, device_id=target, device_id_type=MESH)

    greet({"ctx": sibling})
    greet({"ctx": beside})
    pl.when(has_ahead)(lambda: greet({"ctx": ahead}))
    pl.when(has_behind)(lambda: greet({"ctx": behind}))
    for d in range(1, n_head):
        greet({"head": lax.rem(head + d, n_head)})
    pl.semaphore_wait(
        barrier, n_head + 1 + has_ahead.astype(jnp.int32) + has_behind.astype(jnp.int32)
    )

    def arrive(k, half):
        return (k - 1) * CORES + half + 1

    def send(which, piece, src, dst, index, target):
        return pltpu.make_async_remote_copy(
            src_ref=src, dst_ref=dst,
            send_sem=send_sem.at[which, piece], recv_sem=recv_sem.at[index, piece],
            device_id={"ctx": target}, device_id_type=MESH,
        )

    def slot(k, half, piece):
        return slots.at[k - 1, piece, half]

    def received(k, half, piece):
        place = slot(k, half, piece)
        send(0, piece, place, place, arrive(k, half), sibling).wait_recv()

    sends = []

    def plan(which, src, dst, index, target, cond):
        copies = [send(which, t, src(t), dst(t), index, target) for t in range(PIECES)]
        sends.append((copies, cond))
        return copies

    own_src = lambda t: (k_hbm, v_hbm)[t]
    to_sib = plan(0, own_src, lambda t: sib.at[t], 0, sibling, core == 0)
    to_ahead = plan(1, own_src, lambda t: slot(2, core, t), arrive(2, core), ahead, has_ahead)
    to_side = plan(2, own_src, lambda t: slot(1, core, t), arrive(1, core), beside, side == 0)
    mine2 = lambda t: slot(2, core, t)
    mine1 = lambda t: slot(1, core, t)
    mine3 = lambda t: slot(3, core, t)
    side2even = plan(
        3, mine2, lambda t: slot(3, core, t), arrive(3, core), beside, has_behind & (side == 0)
    )
    side2odd = plan(
        4, mine2, lambda t: slot(1, core, t), arrive(1, core), beside, has_behind & (side == 1)
    )
    sib2 = plan(5, mine2, mine2, arrive(2, core), sibling, has_behind)
    sib1 = plan(6, mine1, mine1, arrive(1, core), sibling, chip >= 1)
    ahead1 = plan(
        7, mine1, lambda t: slot(3, core, t), arrive(3, core), ahead,
        has_behind & (side == 0) & has_ahead,
    )
    sib3 = plan(8, mine3, mine3, arrive(3, core), sibling, chip >= 3)
    conds = {id(c): cond for c, cond in sends}

    def go(copies, t):
        pl.when(conds[id(copies)])(lambda: copies[t].start())

    for t in range(PIECES):
        go(to_sib, t)
        go(to_ahead, t)
        go(to_side, t)

    if part % 128 == 0:
        groups = [(lax.rem(head + d, n_head) * part, part, [d]) for d in range(1, n_head)]
        groups.append((head * part, part, [0]))
    else:
        groups = [(0, rows, list(range(1, n_head)) + [0])]

    def attend(group, get_k, get_v, keys, first, element_mask, row_mask):
        start, count, _ = group
        row = pl.ds(pl.multiple_of(start, 64), count)

        def one(h, carry):
            kv = h // GROUP
            cols = pl.ds(pl.multiple_of(h * HD, HD), HD)
            kv_cols = pl.ds(pl.multiple_of(kv * HD, HD), HD)
            q = q_ref[row, cols]
            s = lax.dot_general(
                q, get_k(kv_cols), (((1,), (1,)), ((), ())), preferred_element_type=jnp.float32
            )
            if element_mask is not None:
                s = jnp.where(element_mask(), s, NEG_FILL)
            peak = jnp.broadcast_to(jnp.max(s, axis=1, keepdims=True), (count, HD))
            if row_mask is not None:
                seen = jnp.broadcast_to(row_mask(), (count, HD))
                peak = jnp.where(seen, peak, NEG_FILL)
            if not first:
                before = top[h, row, :]
                peak = jnp.maximum(before, peak)
            top[h, row, :] = peak
            base = peak
            if row_mask is not None:
                base = jnp.where(seen, peak, POS_FILL)
            p = jnp.exp2(s * SCALE - wide(base * SCALE, keys // HD)).astype(jnp.bfloat16)
            v = get_v(kv_cols)
            v = jnp.concatenate([v, jnp.ones_like(v)], axis=1)
            o = jnp.dot(p, v, preferred_element_type=jnp.float32)
            if not first:
                shrink = jnp.exp2((before - peak) * SCALE)
                o = o + acc[h, row, :] * wide(shrink, 2)
            acc[h, row, :] = o
            return carry

        lax.fori_loop(0, q_heads, one, 0)

    def own_mask(group):
        start, count, _ = group

        def mask():
            i = start + lax.broadcasted_iota(jnp.int32, (count, rows), 0)
            j = lax.broadcasted_iota(jnp.int32, (count, rows), 1)
            doc = doc_ref[pl.ds(pl.multiple_of(start, 64), count), :] - me * rows
            return (j <= i) & (j >= doc)

        return mask

    def sib_mask(group):
        start, count, _ = group

        def mask():
            j = lax.broadcasted_iota(jnp.int32, (count, rows), 1)
            doc = doc_ref[pl.ds(pl.multiple_of(start, 64), count), :] - sibling * rows
            return j >= doc

        return mask

    def slot_mask(group, k):
        start, count, _ = group
        return lambda: doc_ref[pl.ds(pl.multiple_of(start, 64), count), :] <= (chip - k) * CORES * rows

    def attend_slot(group, k):
        def run():
            keys = CORES * rows
            attend(
                group,
                lambda c: slots[k - 1, 0, :, :, c].reshape(keys, HD),
                lambda c: slots[k - 1, 1, :, :, c].reshape(keys, HD),
                keys, False, None, slot_mask(group, k),
            )

        pl.when(chip >= k)(run)

    loads[0].wait()
    loads[1].wait()
    loads[2].wait()
    for group in groups:
        attend(
            group, lambda c: own[0, :, c], lambda c: own[1, :, c], rows, True, own_mask(group), None
        )

    @pl.when(core == 1)
    def _():
        for t in range(PIECES):
            send(0, t, sib.at[t], sib.at[t], 0, sibling).wait_recv()
        for group in groups:
            attend(
                group, lambda c: sib[0, :, c], lambda c: sib[1, :, c], rows, False,
                sib_mask(group), None,
            )

    def relay(k, onward):
        @pl.when(chip >= k)
        def _():
            for t in range(PIECES):
                received(k, core, t)
                for copies in onward:
                    go(copies, t)

    def complete(k):
        @pl.when(chip >= k)
        def _():
            for t in range(PIECES):
                received(k, 1 - core, t)

    relay(2, [side2even, side2odd, sib2])
    relay(1, [ahead1, sib1])
    complete(2)
    for group in groups:
        attend_slot(group, 2)
    relay(3, [sib3])
    complete(1)
    for group in groups:
        attend_slot(group, 1)
    complete(3)
    loads[3].wait()

    pieces = width // chunk

    def parcel(d, n):
        cols = pl.ds(n * chunk, chunk)
        return pltpu.make_async_remote_copy(
            src_ref=outbox.at[d - 1, :, cols], dst_ref=inbox.at[d - 1, :, cols],
            send_sem=psend_sem.at[d - 1, n], recv_sem=precv_sem.at[d - 1, n],
            device_id={"head": lax.rem(head + d, n_head)}, device_id_type=MESH,
        )

    for group in groups:
        attend_slot(group, 3)
        start, count, dests = group
        row = pl.ds(pl.multiple_of(start, 64), count)

        def finish(h, carry):
            cols = pl.ds(pl.multiple_of(h * HD, HD), HD)
            att[row, cols] = (acc[h, row, :HD] / acc[h, row, HD:]).astype(jnp.bfloat16)
            return carry

        lax.fori_loop(0, q_heads, finish, 0)
        for d in dests:
            dest_row = pl.ds(pl.multiple_of(lax.rem(head + d, n_head) * part, 64), part)
            for n in range(pieces):
                cols = pl.ds(n * chunk, chunk)
                total = jnp.dot(
                    att[dest_row, :], w_ref[:, cols], preferred_element_type=jnp.float32
                )
                if d:
                    outbox[d - 1, :, cols] = total.astype(jnp.bfloat16)
                    parcel(d, n).start()
                else:
                    for e in range(1, n_head):
                        parcel(e, n).wait_recv()
                        total = total + inbox[e - 1, :, cols].astype(jnp.float32)
                    out_ref[:, cols] = total.astype(jnp.bfloat16)

    for copies, cond in sends:
        @pl.when(cond)
        def _(copies=copies):
            for copy in copies:
                copy.wait_send()
    for d in range(1, n_head):
        for n in range(pieces):
            parcel(d, n).wait_send()


def on_device(n_ctx, n_head, queries, keys, values, doc_start, out_weight):
    rows, q_width = queries.shape
    kv_width = keys.shape[1]
    width = out_weight.shape[1]
    part = rows // n_head
    q_heads = q_width // HD
    n_slots = LONGEST // SHORT - 1
    chunk = 512
    bf16, f32 = jnp.bfloat16, jnp.float32
    anywhere = pl.BlockSpec(memory_space=pl.ANY)
    vmem = pl.BlockSpec(memory_space=pltpu.VMEM)
    peers = max(n_head - 1, 1)
    return pl.pallas_call(
        functools.partial(kernel, n_ctx, n_head, n_slots, chunk),
        out_shape=jax.ShapeDtypeStruct((part, width), bf16),
        in_specs=[anywhere, anywhere, anywhere, vmem, anywhere],
        out_specs=vmem,
        scratch_shapes=[
            pltpu.VMEM((rows, q_width), bf16),
            pltpu.VMEM((2, rows, kv_width), bf16),
            pltpu.VMEM((2, rows, kv_width), bf16),
            pltpu.VMEM((n_slots, 2, CORES, rows, kv_width), bf16),
            pltpu.VMEM((q_width, width), bf16),
            pltpu.VMEM((q_heads, rows, 2 * HD), f32),
            pltpu.VMEM((q_heads, rows, HD), f32),
            pltpu.VMEM((rows, q_width), bf16),
            pltpu.VMEM((peers, part, width), bf16),
            pltpu.VMEM((peers, part, width), bf16),
            pltpu.SemaphoreType.DMA((4,)),
            pltpu.SemaphoreType.DMA((9, PIECES)),
            pltpu.SemaphoreType.DMA((1 + n_slots * CORES, PIECES)),
            pltpu.SemaphoreType.DMA((peers, width // chunk)),
            pltpu.SemaphoreType.DMA((peers, width // chunk)),
        ],
        compiler_params=pltpu.CompilerParams(
            collective_id=0, has_side_effects=True, vmem_limit_bytes=60 * 1024 * 1024
        ),
    )(queries, keys, values, doc_start.reshape(rows, 1), out_weight)


def solution(mesh):
    return jax.shard_map(
        functools.partial(on_device, mesh.shape["ctx"], mesh.shape["head"]),
        mesh=mesh,
        in_specs=(P("ctx", "head"), P("ctx", "head"), P("ctx", "head"), P("ctx"), P("head", None)),
        out_specs=P(("ctx", "head"), None),
        check_vma=False,
    )
```

time: 513 us -> 171 us (0.33)
  matrix products: 202 us -> 0 us
  waiting for transfers between devices: 181 us -> 0 us
  Pallas kernels: 0 us -> 166 us
  other arithmetic: 94.3 us -> 0 us
  between operations: 14.7 us -> 0.01 us
  local copies, waits for them, and re-layouts: 19.2 us -> 4.66 us
    pallas_call x0 -> x1, Pallas kernels: none -> 166 us  [on_device(): pl.pallas_call(functools.partial(kernel, n_ctx, n_head, n_slots, chunk),...]
    all_gather x1 -> x0, waiting for transfers between devices: 128 us -> none  [on_device(): tile = lax.all_gather(stacked, 'ctx', axis=1, tiled=True)]
    dot_general x2 -> x0, matrix products: 105 us -> none  [the longest x1 91.5 us: compute(): jnp.einsum('tkgd,skd->kgts', queries, key_tile, preferred_element_type=jn...]
    cond x1 -> x0, matrix products: 96.1 us -> none  [attend_block(): return lax.cond(needed, compute, lambda carry: carry, state)]
    reduce_sum x1 -> x0, other arithmetic: 82.6 us -> none  [compute(): total = jnp.sum(weights, axis=-1)]
    reduce_scatter x1 -> x0, waiting for transfers between devices: 53.1 us -> none  [on_device(): lax.psum_scatter(jnp.dot(attended, out_weight, preferred_element_type=jnp...]
    slice x3 -> x0, local copies, waits for them, and re-layouts: 13.4 us -> none  [the longest x1 11.6 us: on_device(): tile[1]]
    and x1 -> x0, other arithmetic: 7.79 us -> none  [compute(): (key_pos[None, :] >= doc_rows[:, None]) & (key_pos[None, :] <= query_pos[...]
  transfers between devices with their start and end apart: 2 -> 0, of which waited for: 2 -> 0; matrix products, arithmetic and copies ran while one was open for 0% -> 0% of each run, Pallas kernels for 0% -> 0%
where the time goes in v1:
time: 171 us
  Pallas kernels  166 us (97%)
  local copies, waits for them, and re-layouts  4.66 us (3%)
    pallas_call x1, Pallas kernels, on_device(): pl.pallas_call(functools.partial(kernel, n_ctx, n_head, n_slots, chunk),...  166 us

profile of v1, /device:TPU:17, one launch (start us, length us, event | category | flops | bytes accessed | tf_op | source)
XLA Modules:
  0.0 170.6 jit_solution(17283298261843094961)
XLA Ops:
  0.0 1.5 copy.6.doc_ref
  1.5 165.9 %shard_map.55 = bf16[256,4096]{1,0:T(8,128)(2,1)} custom-call(bf16[512,2048]{1,0:T(8,128)(2,1)} %q_hbm.1, bf16[512,512]{1,0:T(8,128)(2,1)} %k_hbm.1, bf16[512,512]{1,0:T(8,128)(2,1)} %v_hbm.1, s32[512,1]{1,0:T(8,128)} %copy.6.doc_ref, bf16[2048,4096]{1,0:T(8,128)(2,1)} %w_hbm.1), custom_call_target="tpu_custom_call" | custom-call | tf_op jit(solution)/shard_map/pallas_call | solution.py:309
  167.4 3.1 %copy.8 = bf16[256,4096]{1,0:T(8,128)(2,1)} copy(bf16[256,4096]{1,0:T(8,128)(2,1)} %shard_map.55) | data formatting | bytes 4194304

commit v2 on v1

--- a/solution.py
+++ b/solution.py
@@ -16,7 +16,8 @@
 POS_FILL = 1e30
 SCALE = HD ** -0.5 * 1.4426950408889634
 MESH = pl.DeviceIdType.MESH
-PIECES = 2
+PIECES = 4
+HALVES = PIECES // 2
 
 
 def wide(x, count):
@@ -69,6 +70,11 @@
         barrier, n_head + 1 + has_ahead.astype(jnp.int32) + has_behind.astype(jnp.int32)
     )
 
+    span = rows // HALVES
+
+    def stretch(piece):
+        return pl.ds(piece % HALVES * span, span)
+
     def arrive(k, half):
         return (k - 1) * CORES + half + 1
 
@@ -80,7 +86,7 @@
         )
 
     def slot(k, half, piece):
-        return slots.at[k - 1, piece, half]
+        return slots.at[k - 1, piece // HALVES, half, stretch(piece), :]
 
     def received(k, half, piece):
         place = slot(k, half, piece)
@@ -93,8 +99,9 @@
         sends.append((copies, cond))
         return copies
 
-    own_src = lambda t: (k_hbm, v_hbm)[t]
-    to_sib = plan(0, own_src, lambda t: sib.at[t], 0, sibling, core == 0)
+    own_src = lambda t: (k_hbm, v_hbm)[t // HALVES].at[stretch(t), :]
+    in_sib = lambda t: sib.at[t // HALVES, stretch(t), :]
+    to_sib = plan(0, own_src, in_sib, 0, sibling, core == 0)
     to_ahead = plan(1, own_src, lambda t: slot(2, core, t), arrive(2, core), ahead, has_ahead)
     to_side = plan(2, own_src, lambda t: slot(1, core, t), arrive(1, core), beside, side == 0)
     mine2 = lambda t: slot(2, core, t)
@@ -164,7 +171,7 @@
             acc[h, row, :] = o
             return carry
 
-        lax.fori_loop(0, q_heads, one, 0)
+        lax.fori_loop(0, q_heads, one, 0, unroll=4)
 
     def own_mask(group):
         start, count, _ = group
@@ -203,31 +210,14 @@
 
         pl.when(chip >= k)(run)
 
-    loads[0].wait()
-    loads[1].wait()
-    loads[2].wait()
-    for group in groups:
-        attend(
-            group, lambda c: own[0, :, c], lambda c: own[1, :, c], rows, True, own_mask(group), None
-        )
-
-    @pl.when(core == 1)
-    def _():
-        for t in range(PIECES):
-            send(0, t, sib.at[t], sib.at[t], 0, sibling).wait_recv()
-        for group in groups:
-            attend(
-                group, lambda c: sib[0, :, c], lambda c: sib[1, :, c], rows, False,
-                sib_mask(group), None,
-            )
-
-    def relay(k, onward):
+    def relay(k, t):
+        onward = {1: [ahead1, sib1], 2: [side2even, side2odd, sib2], 3: [sib3]}[k]
+
         @pl.when(chip >= k)
         def _():
-            for t in range(PIECES):
-                received(k, core, t)
-                for copies in onward:
-                    go(copies, t)
+            received(k, core, t)
+            for copies in onward:
+                go(copies, t)
 
     def complete(k):
         @pl.when(chip >= k)
@@ -235,15 +225,51 @@
             for t in range(PIECES):
                 received(k, 1 - core, t)
 
-    relay(2, [side2even, side2odd, sib2])
-    relay(1, [ahead1, sib1])
+    def attend_own(group):
+        attend(
+            group, lambda c: own[0, :, c], lambda c: own[1, :, c], rows, True, own_mask(group), None
+        )
+
+    def attend_sib(group):
+        pl.when(core == 1)(lambda: attend(
+            group, lambda c: sib[0, :, c], lambda c: sib[1, :, c], rows, False,
+            sib_mask(group), None,
+        ))
+
+    early, late = groups[:-1], groups[-1:]
+    loads[0].wait()
+    loads[1].wait()
+    loads[2].wait()
+    for group in groups:
+        attend_own(group)
+    relay(2, 0)
+    relay(2, 1)
+
+    @pl.when(core == 1)
+    def _():
+        for t in range(PIECES):
+            send(0, t, in_sib(t), in_sib(t), 0, sibling).wait_recv()
+
+    for group in early:
+        attend_sib(group)
+    relay(1, 0)
+    relay(2, 2)
+    for group in late:
+        attend_sib(group)
+    relay(1, 1)
+    relay(2, 3)
     complete(2)
-    for group in groups:
+    for group in early:
         attend_slot(group, 2)
-    relay(3, [sib3])
+    relay(1, 2)
+    relay(1, 3)
+    relay(3, 0)
+    relay(3, 1)
     complete(1)
-    for group in groups:
+    for group in early:
         attend_slot(group, 1)
+    relay(3, 2)
+    relay(3, 3)
     complete(3)
     loads[3].wait()
 
@@ -258,6 +284,9 @@
         )
 
     for group in groups:
+        if group is groups[-1]:
+            attend_slot(group, 2)
+            attend_slot(group, 1)
         attend_slot(group, 3)
         start, count, dests = group
         row = pl.ds(pl.multiple_of(start, 64), count)

time: 171 us -> 115 us (0.67)
  Pallas kernels: 166 us -> 110 us
    pallas_call x1, Pallas kernels: 166 us -> 110 us  [on_device(): pl.pallas_call(functools.partial(kernel, n_ctx, n_head, n_slots, chunk),...]
where the time goes in v2:
time: 115 us; the launch traced here: 114 us
  Pallas kernels  110 us (96%)
  local copies, waits for them, and re-layouts  4.66 us (4%)
    pallas_call x1, Pallas kernels, on_device(): pl.pallas_call(functools.partial(kernel, n_ctx, n_head, n_slots, chunk),...  110 us
    unnamed x1, local copies, waits for them, and re-layouts  3.13 us

profile of v2, /device:TPU:17, one launch (start us, length us, event | category | flops | bytes accessed | tf_op | source)
XLA Modules:
  0.0 114.4 jit_solution(16659457054807458617)
XLA Ops:
  0.0 1.5 %copy.6.doc_ref = s32[512,1]{1,0:T(8,128)} copy(s32[512,1]{0,1:T(1,128)} %bitcast.1) | data formatting | bytes 4096 | tf_op jit(solution)/shard_map/reshape | solution.py:363
  1.5 109.8 %shard_map.55 = bf16[256,4096]{1,0:T(8,128)(2,1)} custom-call(bf16[512,2048]{1,0:T(8,128)(2,1)} %q_hbm.1, bf16[512,512]{1,0:T(8,128)(2,1)} %k_hbm.1, bf16[512,512]{1,0:T(8,128)(2,1)} %v_hbm.1, s32[512,1]{1,0:T(8,128)} %copy.6.doc_ref, bf16[2048,4096]{1,0:T(8,128)(2,1)} %w_hbm.1), custom_call_target="tpu_custom_call" | custom-call | tf_op jit(solution)/shard_map/pallas_call | solution.py:338
  111.3 3.1 %copy.8 = bf16[256,4096]{1,0:T(8,128)(2,1)} copy(bf16[256,4096]{1,0:T(8,128)(2,1)} %shard_map.55) | data formatting | bytes 4194304
